TPU v7x, 32 devices: a whole 2x2x4 slice. The times are simulated.
32 devices in a mesh: slab: 8 (over y, x, core), tile: 4 (over z).
Axes of the slice: x: 2, y: 2, z: 4, core: 2. Of those that a mesh axis runs over, the one named last changes fastest.
Arguments:
- field: float32 [64, 64, 1024], P('slab', 'tile'), may hold values from -1 to 1
- dual: float32 [3, 64, 64, 1024], P(None, 'slab', 'tile'), may hold values from -0.5 to 0.5
- depth: float32 [8, 2, 4, 64, 1024], P('slab', None, None, 'tile'), may hold values from 0 to 64
- owner: int32 [2], replicated, may hold values from 0 to 7
- visible: int32 [2, 4, 4], P(None, None, 'tile'), may hold values 0 or 1
Outputs:
- field_out: float32 [64, 64, 1024], P('slab', 'tile')
- dual_out: float32 [3, 64, 64, 1024], P(None, 'slab', 'tile')
All inputs are finite; a program needn't handle non-finite values. No bound on the sum of `visible` on one device may be relied on, other than what follows from the above.
Results may differ from a plain program's by a relative error of at most 0.00002.
Values sent between devices are 32-bit elements; how exact they have to be, the bound alone decides.
A program may use at most 64 MiB of HBM per device.

v0:
```python
import jax
import jax.numpy as jnp
from jax import lax
from jax.sharding import PartitionSpec as P

VIEWS = 4
BINS = 8
BAND = 6
ITERS = 2


def from_root(value, axis, root):
    mine = lax.axis_index(axis) == root
    return lax.psum(jnp.where(mine, value, jnp.zeros_like(value)), axis)


def passed_along(value, axis, steps):
    count = lax.axis_size(axis)
    first, last = (max(0, -steps), min(count, count - steps))
    return lax.ppermute(value, axis, [(source, source + steps) for source in range(first, last)])


def add_votes(histogram, depth_map, seen, zfloat):
    ratio = (depth_map[None, :, :] - zfloat) / float(BAND)
    weight = jnp.clip(ratio + 2.0, 0.0, 1.0) * seen
    place = (jnp.clip(ratio, -1.0, 1.0) + 1.0) * ((BINS - 1) / 2.0)
    return [
        histogram[bin_index] + weight * jnp.maximum(0.0, 1.0 - jnp.abs(place - float(bin_index)))
        for bin_index in range(BINS)
    ]


def proximal(values, histogram):
    total = histogram[0]
    for bin_index in range(1, BINS):
        total = total + histogram[bin_index]
    weights = -total
    best = jnp.minimum(values - 0.05 * weights, -1.0)
    weights = weights + 2.0 * histogram[0]
    for bin_index in range(1, BINS):
        centre = -1.0 + 2.0 * bin_index / (BINS - 1)
        best = jnp.maximum(best, jnp.minimum(values - 0.05 * weights, centre))
        weights = weights + 2.0 * histogram[bin_index]
    return jnp.maximum(best, values - 0.05 * weights)


def dual_step(
    dual_z, dual_x, dual_y, here, ahead_z, ahead_x, zpos, xpos, ypos, total_z, total_x, total_y
):
    zero_y = jnp.zeros(here.shape[:2] + (1,), jnp.float32)
    ahead_y = jnp.concatenate([here[:, :, 1:], zero_y], 2)
    grad_z = jnp.where(zpos < total_z - 1, ahead_z - here, 0.0)
    grad_x = jnp.where(xpos < total_x - 1, ahead_x - here, 0.0)
    grad_y = jnp.where(ypos < total_y - 1, ahead_y - here, 0.0)
    moved_z = dual_z + 0.25 * grad_z
    moved_x = dual_x + 0.25 * grad_x
    moved_y = dual_y + 0.25 * grad_y
    scale = jnp.maximum(1.0, jnp.sqrt(moved_z * moved_z + moved_x * moved_x + moved_y * moved_y))
    inside_z = (zpos >= 0) & (zpos < total_z - 1)
    inside_x = (xpos >= 0) & (xpos < total_x - 1)
    new_z = jnp.where(inside_z, moved_z / scale, 0.0)
    new_x = jnp.where(inside_x, moved_x / scale, 0.0)
    new_y = jnp.where(ypos < total_y - 1, moved_y / scale, 0.0)
    return (new_z, new_x, new_y)


def per_device(field, dual, depth, owner, visible):
    slab_cells, strip_cells, depth_cells = field.shape
    total_z = slab_cells * lax.axis_size("slab")
    total_x = strip_cells * lax.axis_size("tile")
    slab_start = lax.axis_index("slab") * slab_cells
    strip_start = lax.axis_index("tile") * strip_cells
    zpos = slab_start + jnp.arange(slab_cells, dtype=jnp.int32)[:, None, None]
    xpos = strip_start + jnp.arange(strip_cells, dtype=jnp.int32)[None, :, None]
    ypos = jnp.arange(depth_cells, dtype=jnp.int32)[None, None, :]
    zfloat = zpos.astype(jnp.float32)
    histogram = [jnp.zeros(field.shape, jnp.float32) for bin_index in range(BINS)]
    current = field
    dual_z, dual_x, dual_y = (dual[0], dual[1], dual[2])
    extra = field
    zero_y = jnp.zeros((slab_cells, strip_cells, 1), jnp.float32)
    for step_index in range(ITERS):
        batch = from_root(depth[0, step_index], "slab", owner[step_index])
        for view_index in range(VIEWS):
            seen = visible[step_index, view_index, 0].astype(jnp.float32)
            histogram = add_votes(histogram, batch[view_index], seen, zfloat)
        below = passed_along(extra[0:1], "slab", -1)
        beside = passed_along(extra[:, 0:1], "tile", -1)
        ahead_z = jnp.concatenate([extra[1:], below], 0)
        ahead_x = jnp.concatenate([extra[:, 1:], beside], 1)
        dual_z, dual_x, dual_y = dual_step(
            dual_z,
            dual_x,
            dual_y,
            extra,
            ahead_z,
            ahead_x,
            zpos,
            xpos,
            ypos,
            total_z,
            total_x,
            depth_cells,
        )
        above = passed_along(dual_z[-1:], "slab", 1)
        before = passed_along(dual_x[:, -1:], "tile", 1)
        prev_z = jnp.concatenate([above, dual_z[:-1]], 0)
        prev_x = jnp.concatenate([before, dual_x[:, :-1]], 1)
        prev_y = jnp.concatenate([zero_y, dual_y[:, :, :-1]], 2)
        divergence = dual_z - prev_z + (dual_x - prev_x) + (dual_y - prev_y)
        updated = proximal(current + 0.25 * divergence, histogram)
        extra = 2.0 * updated - current
        current = updated
    return (current, jnp.stack([dual_z, dual_x, dual_y]))


def solution(mesh):
    placed = (
        P("slab", "tile", None),
        P(None, "slab", "tile", None),
        P("slab", None, None, "tile", None),
        P(),
        P(None, None, "tile"),
    )
    return jax.shard_map(
        per_device,
        mesh=mesh,
        in_specs=placed,
        out_specs=(P("slab", "tile", None), P(None, "slab", "tile", None)),
        check_vma=False,
    )
```

profile of v0, /device:TPU:0, one launch (start us, length us, event | category | flops | bytes accessed | tf_op | source)
XLA Modules:
  0.0 112.5 jit_solution(6938730917176126711)
XLA Ops:
  7.2 1.0 slice.134
  8.3 1.3 %collective-permute-start.1 = (f32[8,1,1024]{2,1,0:T(1,128)S(1)}, f32[8,1,1024]{2,1,0:T(1,128)S(1)}, u32[]{:S(2)}, u32[]{:S(2)}) collective-permute-start(f32[8,1,1024]{2,1,0:T(1,128)S(1)} %slice.134), channel_id=1, source_target_pairs={{1,0},{2,1},{3,2},{5,4},{6,5},{7,6},{9,8},{10,9},{11,10},{13,12},{... | collective-permute-start | bytes 98312 | tf_op jit(solution)/shard_map/ppermute | solution.py:20
  9.6 0.8 slice.131
  10.4 1.3 %collective-permute-start = (f32[1,16,1024]{2,1,0:T(8,128)S(1)}, f32[1,16,1024]{2,1,0:T(8,128)S(1)}, u32[]{:S(2)}, u32[]{:S(2)}) collective-permute-start(f32[1,16,1024]{2,1,0:T(8,128)S(1)} %slice.131), channel_id=1, source_target_pairs={{4,0},{8,4},{12,8},{16,12},{20,16},{24,20},{28,24},{5,1},{9,5},{13... | collective-permute-start | bytes 196616 | tf_op jit(solution)/shard_map/ppermute | solution.py:20
  11.7 1.3 %fusion.28 = (s32[1]{0:T(128)}, s32[1]{0:T(128)}) fusion(s32[2]{0:T(128)} %param.8), kind=kLoop, calls=%fused_computation.81 | loop fusion | bytes 16 | tf_op jit(solution)/shard_map/slice | solution.py:83
  14.3 1.9 %select_bitcast_fusion = (f32[4,16,1024]{2,1,0:T(8,128)}, f32[4,16,1024]{2,1,0:T(8,128)}) fusion(f32[1,2,4,16,1024]{4,3,2,1,0:T(8,128)} %param.7, pred[]{:T(512)S(6)} %eq.7, pred[]{:T(512)S(6)} %eq.6), kind=kLoop, calls=%fused_computation.62 | loop fusion | flops 131072 | bytes 1048578 | tf_op jit(solution)/shard_map/jit(_where)/select_n | solution.py:14
  16.3 0.7 fusion.27
  17.0 0.2 slice.136
  22.1 2.0 %divide_select_fusion.3 = (f32[8,16,1024]{2,1,0:T(8,128)S(1)}, f32[8,16,1024]{2,1,0:T(8,128)S(1)}, f32[8,16,1024]{2,1,0:T(8,128)S(1)}, f32[8,16,1024]{2,1,0:T(8,128)S(1)}) fusion(pred[1024]{0:T(1024)(128)(4,1)S(1)} %iota_compare_fusion, f32[8,16,1024]{2,1,0:T(8,128)S(1)} %copy-done, f32[1,16,1024]{2,1,0:T(8,128)S(1)} %collective-permute-done, ...), kind=kLoop, calls=%fused_computation.58 | loop fusion | flops 2883584 | bytes 5767704 | tf_op jit(solution)/shard_map/jit(_where)/select_n | solution.py:63
  24.1 0.3 divide_select_fusion.5
  24.5 5.6 %collective-permute-start.3 = (f32[8,1,1024]{2,1,0:T(1,128)S(1)}, f32[8,1,1024]{2,1,0:T(1,128)S(1)}, u32[]{:S(2)}, u32[]{:S(2)}) collective-permute-start(f32[8,1,1024]{2,1,0:T(1,128)S(1)} %slice.174), channel_id=1, source_target_pairs={{0,1},{1,2},{2,3},{4,5},{5,6},{6,7},{8,9},{9,10},{10,11},{12,13},{... | collective-permute-start | bytes 98312 | tf_op jit(solution)/shard_map/ppermute | solution.py:20
  30.1 2.8 %collective-permute-start.2 = (f32[1,16,1024]{2,1,0:T(8,128)S(1)}, f32[1,16,1024]{2,1,0:T(8,128)S(1)}, u32[]{:S(2)}, u32[]{:S(2)}) collective-permute-start(f32[1,16,1024]{2,1,0:T(8,128)S(1)} %slice.172), channel_id=1, source_target_pairs={{0,4},{4,8},{8,12},{12,16},{16,20},{20,24},{24,28},{1,5},{5,9},{9,... | collective-permute-start | bytes 196616 | tf_op jit(solution)/shard_map/ppermute | solution.py:20
  32.9 42.8 %all-reduce.7.cloned.1.call-done = (f32[4,16,1024]{2,1,0:T(8,128)}, f32[4,16,1024]{2,1,0:T(8,128)}) async-done(((f32[4,16,1024]{2,1,0:T(8,128)}, f32[4,16,1024]{2,1,0:T(8,128)}), (f32[4,16,1024]{2,1,0:T(8,128)}, f32[4,16,1024]{2,1,0:T(8,128)})) %all-reduce.7.cloned.1.call-update) | async-done | bytes 524304 | tf_op jit(solution)/shard_map/psum | solution.py:14
  75.6 1.0 slice_bitcast_fusion.7
  76.6 5.0 %multiply_subtract_fusion = (f32[8,16,1024]{2,1,0:T(8,128)S(1)}, f32[8,16,1024]{2,1,0:T(8,128)S(1)}) fusion(f32[8,16,1024]{2,1,0:T(8,128)S(1)} %copy-done, f32[]{:T(128)} %bitcast.12, f32[16,1024]{1,0:T(8,128)S(1)} %get-tuple-element.25, f32[]{:T(128)} %bitcast.10, f32[16,1024]{1,0:T(8,128)S(1)} %get-tuple-element.26, f32[]{:T(128)} %bitcast.8, ...), kind=kLoop, calls=%fused_computation.36 | loop fusion | flops 36831232 | bytes 4980272 | tf_op jit(solution)/shard_map/sub | solution.py:112
  81.7 1.3 %collective-permute-start.5 = (f32[8,1,1024]{2,1,0:T(1,128)S(1)}, f32[8,1,1024]{2,1,0:T(1,128)S(1)}, u32[]{:S(2)}, u32[]{:S(2)}) collective-permute-start(f32[8,1,1024]{2,1,0:T(1,128)S(1)} %slice.184), channel_id=1, source_target_pairs={{1,0},{2,1},{3,2},{5,4},{6,5},{7,6},{9,8},{10,9},{11,10},{13,12},{... | collective-permute-start | bytes 98312 | tf_op jit(solution)/shard_map/ppermute | solution.py:20
  83.0 1.3 %collective-permute-start.4 = (f32[1,16,1024]{2,1,0:T(8,128)S(1)}, f32[1,16,1024]{2,1,0:T(8,128)S(1)}, u32[]{:S(2)}, u32[]{:S(2)}) collective-permute-start(f32[1,16,1024]{2,1,0:T(8,128)S(1)} %slice.182), channel_id=1, source_target_pairs={{4,0},{8,4},{12,8},{16,12},{20,16},{24,20},{28,24},{5,1},{9,5},{13... | collective-permute-start | bytes 196616 | tf_op jit(solution)/shard_map/ppermute | solution.py:20
  84.6 2.9 %collective-permute-done.5 = f32[8,1,1024]{2,1,0:T(1,128)S(1)} collective-permute-done((f32[8,1,1024]{2,1,0:T(1,128)S(1)}, f32[8,1,1024]{2,1,0:T(1,128)S(1)}, u32[]{:S(2)}, u32[]{:S(2)}) %collective-permute-start.5) | collective-permute-done | bytes 32800 | tf_op jit(solution)/shard_map/ppermute | solution.py:20
  87.5 0.6 divide_select_fusion
  88.1 0.2 divide_select_fusion.2
  88.4 3.3 %collective-permute-start.7 = (f32[8,1,1024]{2,1,0:T(1,128)S(1)}, f32[8,1,1024]{2,1,0:T(1,128)S(1)}, u32[]{:S(2)}, u32[]{:S(2)}) collective-permute-start(f32[8,1,1024]{2,1,0:T(1,128)S(1)} %slice.188), channel_id=1, source_target_pairs={{0,1},{1,2},{2,3},{4,5},{5,6},{6,7},{8,9},{9,10},{10,11},{12,13},{... | collective-permute-start | bytes 98312 | tf_op jit(solution)/shard_map/ppermute | solution.py:20
  91.7 3.1 %collective-permute-start.6 = (f32[1,16,1024]{2,1,0:T(8,128)S(1)}, f32[1,16,1024]{2,1,0:T(8,128)S(1)}, u32[]{:S(2)}, u32[]{:S(2)}) collective-permute-start(f32[1,16,1024]{2,1,0:T(8,128)S(1)} %slice.186), channel_id=1, source_target_pairs={{0,4},{4,8},{8,12},{12,16},{16,20},{20,24},{24,28},{1,5},{5,9},{9,... | collective-permute-start | bytes 196616 | tf_op jit(solution)/shard_map/ppermute | solution.py:20
  94.8 1.2 %pad_maximum_fusion = f32[3,8,16,1024]{3,2,1,0:T(8,128)} fusion(f32[1,8,16,1024]{3,2,1,0:T(8,128)S(1)} %bitcast.51, f32[1,8,16,1024]{3,2,1,0:T(8,128)S(1)} %bitcast.47, f32[1,8,16,1024]{3,2,1,0:T(8,128)S(1)} %bitcast.49), kind=kLoop, calls=%fused_computation | loop fusion | flops 786432 | bytes 3145728 | tf_op jit(solution)/shard_map/stack | solution.py:114
  96.1 9.6 %subtract_maximum_fusion = f32[8,16,1024]{2,1,0:T(8,128)} fusion(f32[8,16,1024]{2,1,0:T(8,128)S(1)} %get-tuple-element.9, f32[8,16,1024]{2,1,0:T(8,128)S(1)} %get-tuple-element.17, f32[8,15,1024]{2,1,0:T(8,128)S(1)} %bitcast.48, f32[8,1,1024]{2,1,0:T(1,128)S(1)} %collective-permute-done.7, f32[8,16,1024]{2,1,0:T(8,128)S(1)} %get-tuple-element.16, ...), kind=kLoop, calls=%fused_computation.30 | loop fusion | flops 65404928 | bytes 4718144 | tf_op jit(solution)/shard_map/max | solution.py:44
  (34 shorter events, 0.6 us)
Async XLA Ops:
  7.2 9.8 %copy-start = (f32[8,16,1024]{2,1,0:T(8,128)S(1)}, f32[8,16,1024]{2,1,0:T(8,128)}, u32[]{:S(2)}) copy-start(f32[8,16,1024]{2,1,0:T(8,128)} %param.5) | copy-start | bytes 1572868
  7.2 9.1 %copy-start.2 = (s32[2,4,1]{1,2,0:T(1,128)S(1)}, s32[2,4,1]{1,2,0:T(1,128)}, u32[]{:S(2)}) copy-start(s32[2,4,1]{1,2,0:T(1,128)} %param.9) | copy-start | bytes 100
  7.2 68.4 %all-reduce.7.cloned.1.call-start = ((), (), s32[]{:S(2)}) async-start(), calls=%async_computation | async-start | bytes 1048576 | tf_op jit(solution)/shard_map/psum | solution.py:14
  8.3 13.9 %collective-permute-start.1 = (f32[8,1,1024]{2,1,0:T(1,128)S(1)}, f32[8,1,1024]{2,1,0:T(1,128)S(1)}, u32[]{:S(2)}, u32[]{:S(2)}) collective-permute-start(f32[8,1,1024]{2,1,0:T(1,128)S(1)} %slice.134), channel_id=1, source_target_pairs={{1,0},{2,1},{3,2},{5,4},{6,5},{7,6},{9,8},{10,9},{11,10},{13,12},{... | collective-permute-start | bytes 98312 | tf_op jit(solution)/shard_map/ppermute | solution.py:20
  10.4 11.7 %collective-permute-start = (f32[1,16,1024]{2,1,0:T(8,128)S(1)}, f32[1,16,1024]{2,1,0:T(8,128)S(1)}, u32[]{:S(2)}, u32[]{:S(2)}) collective-permute-start(f32[1,16,1024]{2,1,0:T(8,128)S(1)} %slice.131), channel_id=1, source_target_pairs={{4,0},{8,4},{12,8},{16,12},{20,16},{24,20},{28,24},{5,1},{9,5},{13... | collective-permute-start | bytes 196616 | tf_op jit(solution)/shard_map/ppermute | solution.py:20
  16.2 5.9 %slice-start = ((f32[8,16,1024]{2,1,0:T(8,128)}), f32[7,16,1024]{2,1,0:T(8,128)S(1)}, s32[]{:S(2)}) async-start(f32[8,16,1024]{2,1,0:T(8,128)} %param.5), calls=%async_computation.1 | async-start | bytes 917504 | tf_op jit(solution)/shard_map/slice | solution.py:89
  24.5 52.1 %collective-permute-start.3 = (f32[8,1,1024]{2,1,0:T(1,128)S(1)}, f32[8,1,1024]{2,1,0:T(1,128)S(1)}, u32[]{:S(2)}, u32[]{:S(2)}) collective-permute-start(f32[8,1,1024]{2,1,0:T(1,128)S(1)} %slice.174), channel_id=1, source_target_pairs={{0,1},{1,2},{2,3},{4,5},{5,6},{6,7},{8,9},{9,10},{10,11},{12,13},{... | collective-permute-start | bytes 98312 | tf_op jit(solution)/shard_map/ppermute | solution.py:20
  30.1 46.5 %collective-permute-start.2 = (f32[1,16,1024]{2,1,0:T(8,128)S(1)}, f32[1,16,1024]{2,1,0:T(8,128)S(1)}, u32[]{:S(2)}, u32[]{:S(2)}) collective-permute-start(f32[1,16,1024]{2,1,0:T(8,128)S(1)} %slice.172), channel_id=1, source_target_pairs={{0,4},{4,8},{8,12},{12,16},{16,20},{20,24},{24,28},{1,5},{5,9},{9,... | collective-permute-start | bytes 196616 | tf_op jit(solution)/shard_map/ppermute | solution.py:20
  76.6 7.7 %copy-start.1 = (f32[4,16,1024]{2,1,0:T(8,128)S(1)}, f32[4,16,1024]{2,1,0:T(8,128)}, u32[]{:S(2)}) copy-start(f32[4,16,1024]{2,1,0:T(8,128)} %get-tuple-element.3) | copy-start | bytes 786436
  81.7 5.8 %collective-permute-start.5 = (f32[8,1,1024]{2,1,0:T(1,128)S(1)}, f32[8,1,1024]{2,1,0:T(1,128)S(1)}, u32[]{:S(2)}, u32[]{:S(2)}) collective-permute-start(f32[8,1,1024]{2,1,0:T(1,128)S(1)} %slice.184), channel_id=1, source_target_pairs={{1,0},{2,1},{3,2},{5,4},{6,5},{7,6},{9,8},{10,9},{11,10},{13,12},{... | collective-permute-start | bytes 98312 | tf_op jit(solution)/shard_map/ppermute | solution.py:20
  83.0 4.5 %collective-permute-start.4 = (f32[1,16,1024]{2,1,0:T(8,128)S(1)}, f32[1,16,1024]{2,1,0:T(8,128)S(1)}, u32[]{:S(2)}, u32[]{:S(2)}) collective-permute-start(f32[1,16,1024]{2,1,0:T(8,128)S(1)} %slice.182), channel_id=1, source_target_pairs={{4,0},{8,4},{12,8},{16,12},{20,16},{24,20},{28,24},{5,1},{9,5},{13... | collective-permute-start | bytes 196616 | tf_op jit(solution)/shard_map/ppermute | solution.py:20
  88.4 7.7 %collective-permute-start.7 = (f32[8,1,1024]{2,1,0:T(1,128)S(1)}, f32[8,1,1024]{2,1,0:T(1,128)S(1)}, u32[]{:S(2)}, u32[]{:S(2)}) collective-permute-start(f32[8,1,1024]{2,1,0:T(1,128)S(1)} %slice.188), channel_id=1, source_target_pairs={{0,1},{1,2},{2,3},{4,5},{5,6},{6,7},{8,9},{9,10},{10,11},{12,13},{... | collective-permute-start | bytes 98312 | tf_op jit(solution)/shard_map/ppermute | solution.py:20
  91.7 4.4 %collective-permute-start.6 = (f32[1,16,1024]{2,1,0:T(8,128)S(1)}, f32[1,16,1024]{2,1,0:T(8,128)S(1)}, u32[]{:S(2)}, u32[]{:S(2)}) collective-permute-start(f32[1,16,1024]{2,1,0:T(8,128)S(1)} %slice.186), channel_id=1, source_target_pairs={{0,4},{4,8},{8,12},{12,16},{16,20},{20,24},{24,28},{1,5},{5,9},{9,... | collective-permute-start | bytes 196616 | tf_op jit(solution)/shard_map/ppermute | solution.py:20
Sparse Core Ops, SparseCore 0:
  16.3 59.2 all-reduce.6
where the time goes:
time: 113 us
  waiting for transfers between devices  45.7 us (40%)
  other arithmetic  20.9 us (18%)
  between operations  20.5 us (18%)
  starting transfers between devices  19.9 us (18%)
  local copies, waits for them, and re-layouts  5.55 us (5%)
    psum x1, waiting for transfers between devices, from_root(): return lax.psum(jnp.where(mine, value, jnp.zeros_like(value)), axis)  42.8 us
    ppermute x8, starting transfers between devices, passed_along(): lax.ppermute(value, axis, [(source, source + steps) for source in range(f...  19.8 us
    max x1, other arithmetic, proximal(): return jnp.maximum(best, values - 0.05 * weights)  9.61 us
    sub x1, other arithmetic, per_device(): extra = 2.0 * updated - current  5.02 us
    ppermute x8, waiting for transfers between devices, passed_along(): lax.ppermute(value, axis, [(source, source + steps) for source in range(f...  2.89 us
    select_n x2, other arithmetic, dual_step(): new_y = jnp.where(ypos < total_y - 1, moved_y / scale, 0.0)  2.54 us
  transfers between devices with their start and end apart: 9, of which 2 were waited for; matrix products, arithmetic and copies ran while one was open for 9% of the time, Pallas kernels for 0%

commit v1 on v0

v1 whole, which is shorter than its diff:
```python
import functools

import jax
import jax.numpy as jnp
from jax import lax
from jax.experimental import pallas as pl
from jax.experimental.pallas import tpu as pltpu
from jax.sharding import PartitionSpec as P

VIEWS = 4
BINS = 8
BAND = 6
ITERS = 2

ROWS = 8
UNIT = 0.35
HALF = VIEWS // 2
MESH = pl.DeviceIdType.MESH


def kernel(
    n_slab,
    n_tile,
    owner_ref,
    visible_ref,
    field_ref,
    dual_ref,
    depth_ref,
    field_out,
    dual_out,
    extra,
    start_p,
    dual_z,
    dual_x,
    dual_y,
    part,
    value,
    votes,
    mine,
    got,
    kept,
    batch,
    row_send,
    row_recv,
    depth_send,
    depth_recv,
    halo_send,
    halo_recv,
    local_sem,
):
    nz, nx, ny = field_ref.shape
    groups = nx // ROWS
    chunk = min(256, ny)
    chunks = ny // chunk
    slab = lax.axis_index("slab")
    tile = lax.axis_index("tile")
    bits = []
    while 2 ** len(bits) < n_slab:
        bits.append(len(bits))
    middle = bits[1:]
    order = (middle, middle[::-1])
    last = len(middle) + 1
    side = [lax.rem(lax.div(slab, 2**b), 2) for b in bits]
    partner = [slab + 2**b * (1 - 2 * side[b]) for b in bits]
    core = side[0]
    first_slab, last_slab = slab == 0, slab == n_slab - 1
    first_tile, last_tile = tile == 0, tile == n_tile - 1

    into_field = pltpu.make_async_copy(
        field_ref, extra.at[0, pl.ds(0, nz), pl.ds(0, nx)], local_sem.at[0]
    )
    into_dual = pltpu.make_async_copy(dual_ref, start_p, local_sem.at[1])
    into_mine = [
        pltpu.make_async_copy(
            depth_ref.at[0, k, pl.ds(HALF * core, HALF)], mine.at[k], local_sem.at[2 + k]
        )
        for k in range(ITERS)
    ]
    into_field.start()
    into_mine[0].start()
    into_mine[1].start()
    into_dual.start()

    barrier = pltpu.get_barrier_semaphore()
    for b in bits:
        pl.semaphore_signal(
            barrier, inc=1, device_id={"slab": partner[b]}, device_id_type=MESH
        )
    greeted = len(bits)
    for axis, place, here, there in (
        ("slab", slab, first_slab, -1),
        ("slab", slab, last_slab, 1),
        ("tile", tile, first_tile, -1),
        ("tile", tile, last_tile, 1),
    ):

        @pl.when(jnp.logical_not(here))
        def _(axis=axis, place=place, there=there):
            pl.semaphore_signal(
                barrier, inc=1, device_id={axis: place + there}, device_id_type=MESH
            )

    inner = [jnp.where(edge, 0, 1) for edge in (first_slab, last_slab, first_tile, last_tile)]
    pl.semaphore_wait(barrier, greeted + inner[0] + inner[1] + inner[2] + inner[3])

    def exchange(k, stage, piece, source, target, b):
        return pltpu.make_async_remote_copy(
            src_ref=source,
            dst_ref=target,
            send_sem=depth_send.at[k, stage, piece],
            recv_sem=depth_recv.at[k, stage, piece],
            device_id={"slab": partner[b]},
            device_id_type=MESH,
        )

    def first_copy(k):
        return exchange(
            k,
            0,
            0,
            depth_ref.at[0, k, pl.ds(HALF * (1 - core), HALF)],
            got.at[k, 0],
            0,
        )

    def middle_copy(k, stage, piece):
        return exchange(
            k,
            stage,
            piece,
            kept.at[k, stage - 1, piece],
            got.at[k, stage, piece],
            order[piece][stage - 1],
        )

    def last_copy(k):
        there = batch.at[k, pl.ds(HALF * core, HALF)]
        return exchange(k, last, 0, there, there, 0)

    def owned(k, b):
        return lax.rem(lax.div(owner_ref[k], 2**b), 2) == side[b]

    def scaled(k, piece, depth):
        seen = jnp.where(core == 0, visible_ref[k, piece, 0], visible_ref[k, HALF + piece, 0])
        return jnp.where(seen == 1, depth * (UNIT / BAND) + 2.0 * UNIT, -1e6)

    def keep(k, stage, piece, chosen):
        if stage < last - 1:
            kept[k, stage, piece] = chosen
        else:
            batch[k, HALF * core + piece] = scaled(k, piece, chosen)

    def forward(k, stage, piece):
        if stage == 0:
            keep(k, 0, piece, jnp.where(owned(k, 0), mine[k, piece], got[k, 0, piece]))
        else:
            b = order[piece][stage - 1]
            keep(
                k,
                stage,
                piece,
                jnp.where(owned(k, b), kept[k, stage - 1, piece], got[k, stage, piece]),
            )

    def pass_on(k, stage):
        if stage == 0:
            into_mine[k].wait()
            first_copy(k).wait_recv()
        for piece in range(2):
            if stage > 0:
                middle_copy(k, stage, piece).wait_recv()
            forward(k, stage, piece)
            if stage < last - 1:
                middle_copy(k, stage + 1, piece).start()
        if stage == last - 1:
            last_copy(k).start()

    def halo(it, kind):
        if kind == 0:
            source, target = extra.at[it, 0, pl.ds(0, nx)], extra.at[it, nz, pl.ds(0, nx)]
            device = {"slab": slab - 1}
        elif kind == 1:
            source, target = row_send.at[it, 0], row_recv.at[it, 0]
            device = {"tile": tile - 1}
        elif kind == 2:
            source, target = dual_z.at[it, nz], dual_z.at[it, 0]
            device = {"slab": slab + 1}
        else:
            source, target = row_send.at[it, 1], row_recv.at[it, 1]
            device = {"tile": tile + 1}
        return pltpu.make_async_remote_copy(
            src_ref=source,
            dst_ref=target,
            send_sem=halo_send.at[it, kind],
            recv_sem=halo_recv.at[it, kind],
            device_id=device,
            device_id_type=MESH,
        )

    sends_not = (first_slab, first_tile, last_slab, last_tile)
    gets_not = (last_slab, last_tile, first_slab, first_tile)

    def send_halo(it, kind):
        @pl.when(jnp.logical_not(sends_not[kind]))
        def _():
            halo(it, kind).start()

    def sent_halo(it, kind):
        @pl.when(jnp.logical_not(sends_not[kind]))
        def _():
            halo(it, kind).wait_send()

    def take_halo(it, kind):
        @pl.when(jnp.logical_not(gets_not[kind]))
        def _():
            halo(it, kind).wait_recv()
            for z in range(nz):
                if kind == 1:
                    extra[it, z, nx : nx + 1, :] = row_recv[it, 0, z : z + 1, :]
                if kind == 3:
                    dual_x[it, z, ROWS - 1 : ROWS, :] = row_recv[it, 1, z : z + 1, :]

        @pl.when(gets_not[kind])
        def _():
            if kind == 0:
                extra[it, nz, 0:nx, :] = jnp.zeros((nx, ny), jnp.float32)
            if kind == 2:
                dual_z[it, 0] = jnp.zeros((nx, ny), jnp.float32)
            for z in range(nz):
                if kind == 1:
                    extra[it, z, nx : nx + 1, :] = jnp.zeros((1, ny), jnp.float32)
                if kind == 3:
                    dual_x[it, z, ROWS - 1 : ROWS, :] = jnp.zeros((1, ny), jnp.float32)

    def pack_extra(it):
        for z in range(nz):
            row_send[it, 0, z : z + 1, :] = extra[it, z, 0:1, :]

    def pack_dual(it):
        for z in range(nz):
            row_send[it, 1, z : z + 1, :] = dual_x[it, z, ROWS + nx - 1 : ROWS + nx, :]

    def dual_pass(it, group, low, high):
        row = ROWS * group
        lane = lax.broadcasted_iota(jnp.int32, (ROWS, ny), 1)
        inside_y = jnp.where(lane < ny - 1, 1.0, 0.0)
        rows = lax.broadcasted_iota(jnp.int32, (ROWS, ny), 0) + (tile * nx + row)
        inside_x = jnp.where(rows < nx * n_tile - 1, 1.0, 0.0)

        def body(z, carry):
            inside_z = jnp.where(slab * nz + z < nz * n_slab - 1, 1.0, 0.0)
            here = extra[it, z, row : row + ROWS, :]
            ahead_z = extra[it, z + 1, row : row + ROWS, :]
            ahead_x = extra[it, z, row + 1 : row + 1 + ROWS, :]
            ahead_y = pltpu.roll(here, ny - 1, 1)
            if it == 0:
                old_z = start_p[0, z, row : row + ROWS, :]
                old_x = start_p[1, z, row : row + ROWS, :]
                old_y = start_p[2, z, row : row + ROWS, :]
                current = here
            else:
                old_z = dual_z[it - 1, z + 1, row : row + ROWS, :]
                old_x = dual_x[it - 1, z, ROWS + row : ROWS + row + ROWS, :]
                old_y = dual_y[it - 1, z, row : row + ROWS, :]
                current = value[it - 1, z, row : row + ROWS, :]
            moved_z = old_z + (0.25 * inside_z) * (ahead_z - here)
            moved_x = old_x + (0.25 * inside_x) * (ahead_x - here)
            moved_y = old_y + (0.25 * inside_y) * (ahead_y - here)
            size = moved_z * moved_z + moved_x * moved_x + moved_y * moved_y
            scale = lax.rsqrt(jnp.maximum(size, 1.0))
            new_y = moved_y * (scale * inside_y)
            dual_z[it, z + 1, row : row + ROWS, :] = moved_z * (scale * inside_z)
            dual_x[it, z, ROWS + row : ROWS + row + ROWS, :] = moved_x * (scale * inside_x)
            dual_y[it, z, row : row + ROWS, :] = new_y
            part[z, row : row + ROWS, :] = current + 0.25 * (new_y - pltpu.roll(new_y, 1, 1))
            return carry

        lax.fori_loop(low, high, body, 0)

    def over(low, high, body):
        def step(i, carry):
            z = low + lax.div(i, chunks)
            body(z, pl.ds(pl.multiple_of(lax.rem(i, chunks) * chunk, chunk), chunk))
            return carry

        lax.fori_loop(0, (high - low) * chunks, step, 0)

    def add_votes(k, z, rows, lanes, sums):
        shift = (slab * nz + z).astype(jnp.float32) * (UNIT / BAND)
        for view in range(VIEWS):
            reach = jnp.maximum(batch[k, view, rows, lanes] - shift, 0.0)
            clipped = [jnp.minimum(reach, UNIT + 0.1 * i) for i in range(BINS)]
            sums = clipped if sums is None else [s + c for s, c in zip(sums, clipped)]
        return sums

    def votes_pass(k, group, low, high):
        rows = pl.ds(ROWS * group, ROWS)

        def body(z, lanes):
            sums = add_votes(k, z, rows, lanes, [votes[i, z, rows, lanes] for i in range(BINS)])
            for i in range(BINS):
                votes[i, z, rows, lanes] = sums[i]

        over(low, high, body)

    def field_pass(it, group, low, high):
        row = ROWS * group
        rows = pl.ds(row, ROWS)

        def body(z, lanes):
            if it == 0:
                sums = add_votes(0, z, rows, lanes, None)
                for i in range(BINS):
                    votes[i, z, rows, lanes] = sums[i]
            else:
                sums = [votes[i, z, rows, lanes] for i in range(BINS)]
            moved = dual_z[it, z + 1, rows, lanes] - dual_z[it, z, rows, lanes]
            moved = moved + (
                dual_x[it, z, pl.ds(ROWS + row, ROWS), lanes]
                - dual_x[it, z, pl.ds(ROWS + row - 1, ROWS), lanes]
            )
            values = part[z, rows, lanes] + 0.25 * moved
            total = sums[0] * (0.05 / UNIT)
            base = values - total
            best = jnp.maximum(base, jnp.minimum(values + total, -1.0))
            for i in range(1, BINS):
                centre = -1.0 + 2.0 * i / (BINS - 1)
                best = jnp.maximum(
                    best, jnp.minimum(base + (sums[i] - sums[i - 1]), centre)
                )
            value[it, z, rows, lanes] = best
            if it == 0:
                extra[1, z, rows, lanes] = 2.0 * best - extra[0, z, rows, lanes]

        over(low, high, body)

    for k in range(ITERS):
        first_copy(k).start()
    into_field.wait()
    send_halo(0, 0)
    pack_extra(0)
    send_halo(0, 1)
    pass_on(0, 0)
    pass_on(1, 0)
    into_dual.wait()
    for group in range(groups - 1):
        dual_pass(0, group, 0, nz - 1)
    take_halo(0, 0)
    take_halo(0, 1)
    for stage in range(1, last - 1):
        pass_on(0, stage)
    for group in range(groups):
        dual_pass(0, group, nz - 1, nz)
    send_halo(0, 2)
    dual_pass(0, groups - 1, 0, nz - 1)
    pack_dual(0)
    send_halo(0, 3)
    for stage in range(1, last - 1):
        pass_on(1, stage)
    if last > 1:
        pass_on(0, last - 1)
    take_halo(0, 2)
    take_halo(0, 3)
    last_copy(0).wait_recv()

    for group in range(groups):
        field_pass(0, group, 0, 1)
    send_halo(1, 0)
    field_pass(0, 0, 1, nz)
    pack_extra(1)
    send_halo(1, 1)
    if last > 1:
        pass_on(1, last - 1)
    for group in range(1, groups):
        field_pass(0, group, 1, nz)
    for group in range(groups - 1):
        dual_pass(1, group, 0, nz - 1)
    last_copy(1).wait_recv()
    votes_pass(1, groups - 1, 0, nz)
    take_halo(1, 0)
    take_halo(1, 1)
    for group in range(groups):
        dual_pass(1, group, nz - 1, nz)
    send_halo(1, 2)
    dual_pass(1, groups - 1, 0, nz - 1)
    pack_dual(1)
    send_halo(1, 3)
    out_dual = [
        pltpu.make_async_copy(
            dual_z.at[1, pl.ds(1, nz)], dual_out.at[0], local_sem.at[4]
        ),
        pltpu.make_async_copy(
            dual_x.at[1, pl.ds(0, nz), pl.ds(ROWS, nx)], dual_out.at[1], local_sem.at[5]
        ),
        pltpu.make_async_copy(dual_y.at[1], dual_out.at[2], local_sem.at[6]),
    ]
    for copy in out_dual:
        copy.start()
    for group in range(groups - 1):
        votes_pass(1, group, 0, nz)
    for group in range(1, groups):
        field_pass(1, group, 1, nz)
    take_halo(1, 2)
    take_halo(1, 3)
    for group in range(groups):
        field_pass(1, group, 0, 1)
    field_pass(1, 0, 1, nz)
    out_field = pltpu.make_async_copy(value.at[1], field_out, local_sem.at[7])
    out_field.start()

    for k in range(ITERS):
        first_copy(k).wait_send()
        for stage in range(1, last):
            for piece in range(2):
                middle_copy(k, stage, piece).wait_send()
        last_copy(k).wait_send()
    for it in range(ITERS):
        for kind in range(4):
            sent_halo(it, kind)
    for copy in out_dual:
        copy.wait()
    out_field.wait()


def per_device(n_slab, n_tile, field, dual, depth, owner, visible):
    nz, nx, ny = field.shape
    stages = 1
    while 2**stages < n_slab:
        stages += 1
    slots = stages + 1
    f32 = jnp.float32
    anywhere = pl.BlockSpec(memory_space=pl.ANY)
    scalars = pl.BlockSpec(memory_space=pltpu.SMEM)
    return pl.pallas_call(
        functools.partial(kernel, n_slab, n_tile),
        out_shape=(
            jax.ShapeDtypeStruct(field.shape, f32),
            jax.ShapeDtypeStruct(dual.shape, f32),
        ),
        in_specs=[scalars, scalars, anywhere, anywhere, anywhere],
        out_specs=(anywhere, anywhere),
        scratch_shapes=[
            pltpu.VMEM((ITERS, nz + 1, nx + 8, ny), f32),
            pltpu.VMEM((3, nz, nx, ny), f32),
            pltpu.VMEM((ITERS, nz + 1, nx, ny), f32),
            pltpu.VMEM((ITERS, nz, nx + 8, ny), f32),
            pltpu.VMEM((ITERS, nz, nx, ny), f32),
            pltpu.VMEM((nz, nx, ny), f32),
            pltpu.VMEM((ITERS, nz, nx, ny), f32),
            pltpu.VMEM((BINS, nz, nx, ny), f32),
            pltpu.VMEM((ITERS, HALF, nx, ny), f32),
            pltpu.VMEM((ITERS, slots, HALF, nx, ny), f32),
            pltpu.VMEM((ITERS, slots, HALF, nx, ny), f32),
            pltpu.VMEM((ITERS, VIEWS, nx, ny), f32),
            pltpu.VMEM((ITERS, 2, nz, ny), f32),
            pltpu.VMEM((ITERS, 2, nz, ny), f32),
            pltpu.SemaphoreType.DMA((ITERS, slots, 2)),
            pltpu.SemaphoreType.DMA((ITERS, slots, 2)),
            pltpu.SemaphoreType.DMA((ITERS, 4)),
            pltpu.SemaphoreType.DMA((ITERS, 4)),
            pltpu.SemaphoreType.DMA((8,)),
        ],
        compiler_params=pltpu.CompilerParams(
            collective_id=0, has_side_effects=True, vmem_limit_bytes=40 * 2**20
        ),
        name="merge",
    )(owner, visible, field, dual, depth)


def solution(mesh):
    placed = (
        P("slab", "tile", None),
        P(None, "slab", "tile", None),
        P("slab", None, None, "tile", None),
        P(),
        P(None, None, "tile"),
    )
    return jax.shard_map(
        functools.partial(per_device, mesh.shape["slab"], mesh.shape["tile"]),
        mesh=mesh,
        in_specs=placed,
        out_specs=(P("slab", "tile", None), P(None, "slab", "tile", None)),
        check_vma=False,
    )
```

time: 113 us -> 31.6 us (0.28)
  the two profiles are of different devices: /device:TPU:0 before, /device:TPU:1 now
where the time goes in v1:
time: 31.6 us; the launch traced here: 31.4 us
  Pallas kernels  23.9 us (76%)
  local copies, waits for them, and re-layouts  6.85 us (22%)
  between operations  0.64 us (2%)
    pallas_call x1, Pallas kernels, per_device(): pl.pallas_call(functools.partial(kernel, n_slab, n_tile), out_shape=(jax....  23.9 us
    unnamed x11, local copies, waits for them, and re-layouts  6.85 us

profile of v1, /device:TPU:1, one launch (start us, length us, event | category | flops | bytes accessed | tf_op | source)
XLA Modules:
  0.0 31.4 jit_solution(59484586679360273)
XLA Ops:
  0.6 0.8 %copy.7.visible_ref = s32[2,4,1]{2,1,0:T(4,128)S(1)} copy(s32[2,4,1]{1,2,0:T(1,128)} %param.9) | data formatting | bytes 64 | tf_op args[4]
  1.4 0.0 copy-start
  1.4 1.4 %copy-done = f32[3,8,16,1024]{3,2,1,0:T(8,128)S(1)} copy-done((f32[3,8,16,1024]{3,2,1,0:T(8,128)S(1)}, f32[3,8,16,1024]{3,2,1,0:T(8,128)}, u32[]{:S(2)}) %copy-start) | copy-done | bytes 1572888
  2.8 0.0 copy-start.1
  2.8 1.0 %copy-done.1 = f32[8,16,1024]{2,1,0:T(8,128)S(1)} copy-done((f32[8,16,1024]{2,1,0:T(8,128)S(1)}, f32[8,16,1024]{2,1,0:T(8,128)}, u32[]{:S(2)}) %copy-start.1) | copy-done | bytes 524312
  3.9 0.0 copy-start.2
  3.9 1.0 %copy-done.2 = f32[1,2,4,16,1024]{4,3,2,1,0:T(8,128)S(1)} copy-done((f32[1,2,4,16,1024]{4,3,2,1,0:T(8,128)S(1)}, f32[1,2,4,16,1024]{4,3,2,1,0:T(8,128)}, u32[]{:S(2)}) %copy-start.2) | copy-done | bytes 524312
  4.9 0.0 copy-start.3
  4.9 0.7 %copy-done.3 = s32[2]{0:T(128)S(1)} copy-done((s32[2]{0:T(128)S(1)}, s32[2]{0:T(128)}, u32[]{:S(2)}) %copy-start.3) | copy-done | bytes 32
  5.5 23.9 %merge.1 = (f32[8,16,1024]{2,1,0:T(8,128)S(1)}, f32[3,8,16,1024]{3,2,1,0:T(8,128)S(1)}) custom-call(s32[2]{0:T(128)S(1)} %copy-done.3, s32[2,4,1]{2,1,0:T(4,128)S(1)} %copy.7.visible_ref, f32[8,16,1024]{2,1,0:T(8,128)S(1)} %copy-done.1, f32[3,8,16,1024]{3,2,1,0:T(8,128)S(1)} %copy-done, f32[1,2,4,16,1024]{4,3,2,1,0:T(8,128)S(1)} %copy-done.2), custom_call_target="tpu_custom_call" | custom-call | tf_op jit(solution)/shard_map/merge/pallas_call | solution.py:434
  29.4 0.8 %copy.10 = f32[8,16,1024]{2,1,0:T(8,128)} copy(f32[8,16,1024]{2,1,0:T(8,128)S(1)} %get-tuple-element.4) | data formatting | bytes 1048576
  30.2 1.1 %copy.11 = f32[3,8,16,1024]{3,2,1,0:T(8,128)} copy(f32[3,8,16,1024]{3,2,1,0:T(8,128)S(1)} %get-tuple-element.5) | data formatting | bytes 3145728
Async XLA Ops:
  1.4 1.4 %copy-start = (f32[3,8,16,1024]{3,2,1,0:T(8,128)S(1)}, f32[3,8,16,1024]{3,2,1,0:T(8,128)}, u32[]{:S(2)}) copy-start(f32[3,8,16,1024]{3,2,1,0:T(8,128)} %dual_ref.1) | copy-start | bytes 4718596
  2.8 1.0 %copy-start.1 = (f32[8,16,1024]{2,1,0:T(8,128)S(1)}, f32[8,16,1024]{2,1,0:T(8,128)}, u32[]{:S(2)}) copy-start(f32[8,16,1024]{2,1,0:T(8,128)} %field_ref.1) | copy-start | bytes 1572868
  3.9 1.0 %copy-start.2 = (f32[1,2,4,16,1024]{4,3,2,1,0:T(8,128)S(1)}, f32[1,2,4,16,1024]{4,3,2,1,0:T(8,128)}, u32[]{:S(2)}) copy-start(f32[1,2,4,16,1024]{4,3,2,1,0:T(8,128)} %depth_ref.1) | copy-start | bytes 1572868
  4.9 0.7 %copy-start.3 = (s32[2]{0:T(128)S(1)}, s32[2]{0:T(128)}, u32[]{:S(2)}) copy-start(s32[2]{0:T(128)} %owner_ref.1) | copy-start | bytes 28

commit v2 on v1

--- a/solution.py
+++ b/solution.py
@@ -21,8 +21,8 @@
 def kernel(
     n_slab,
     n_tile,
-    owner_ref,
-    visible_ref,
+    owner_in,
+    visible_in,
     field_ref,
     dual_ref,
     depth_ref,
@@ -47,10 +47,12 @@
     halo_send,
     halo_recv,
     local_sem,
+    owner_ref,
+    visible_ref,
 ):
     nz, nx, ny = field_ref.shape
     groups = nx // ROWS
-    chunk = min(256, ny)
+    chunk = min(512, ny)
     chunks = ny // chunk
     slab = lax.axis_index("slab")
     tile = lax.axis_index("tile")
@@ -76,8 +78,12 @@
         )
         for k in range(ITERS)
     ]
+    into_owner = pltpu.make_async_copy(owner_in, owner_ref, local_sem.at[8])
+    into_visible = pltpu.make_async_copy(visible_in, visible_ref, local_sem.at[9])
+    into_owner.start()
+    into_visible.start()
+    into_mine[0].start()
     into_field.start()
-    into_mine[0].start()
     into_mine[1].start()
     into_dual.start()
 
@@ -141,7 +147,9 @@
         return lax.rem(lax.div(owner_ref[k], 2**b), 2) == side[b]
 
     def scaled(k, piece, depth):
-        seen = jnp.where(core == 0, visible_ref[k, piece, 0], visible_ref[k, HALF + piece, 0])
+        seen = jnp.where(
+            core == 0, visible_ref[k, 0, piece], visible_ref[k, 0, HALF + piece]
+        )
         return jnp.where(seen == 1, depth * (UNIT / BAND) + 2.0 * UNIT, -1e6)
 
     def keep(k, stage, piece, chosen):
@@ -293,16 +301,6 @@
             sums = clipped if sums is None else [s + c for s, c in zip(sums, clipped)]
         return sums
 
-    def votes_pass(k, group, low, high):
-        rows = pl.ds(ROWS * group, ROWS)
-
-        def body(z, lanes):
-            sums = add_votes(k, z, rows, lanes, [votes[i, z, rows, lanes] for i in range(BINS)])
-            for i in range(BINS):
-                votes[i, z, rows, lanes] = sums[i]
-
-        over(low, high, body)
-
     def field_pass(it, group, low, high):
         row = ROWS * group
         rows = pl.ds(row, ROWS)
@@ -313,7 +311,8 @@
                 for i in range(BINS):
                     votes[i, z, rows, lanes] = sums[i]
             else:
-                sums = [votes[i, z, rows, lanes] for i in range(BINS)]
+                before = [votes[i, z, rows, lanes] for i in range(BINS)]
+                sums = add_votes(1, z, rows, lanes, before)
             moved = dual_z[it, z + 1, rows, lanes] - dual_z[it, z, rows, lanes]
             moved = moved + (
                 dual_x[it, z, pl.ds(ROWS + row, ROWS), lanes]
@@ -334,29 +333,29 @@
 
         over(low, high, body)
 
-    for k in range(ITERS):
-        first_copy(k).start()
+    first_copy(0).start()
     into_field.wait()
+    pack_extra(0)
+    into_owner.wait()
+    into_visible.wait()
+    pass_on(0, 0)
     send_halo(0, 0)
-    pack_extra(0)
     send_halo(0, 1)
-    pass_on(0, 0)
-    pass_on(1, 0)
+    first_copy(1).start()
     into_dual.wait()
     for group in range(groups - 1):
         dual_pass(0, group, 0, nz - 1)
+    for stage in range(1, last - 1):
+        pass_on(0, stage)
     take_halo(0, 0)
     take_halo(0, 1)
-    for stage in range(1, last - 1):
-        pass_on(0, stage)
     for group in range(groups):
         dual_pass(0, group, nz - 1, nz)
     send_halo(0, 2)
     dual_pass(0, groups - 1, 0, nz - 1)
     pack_dual(0)
     send_halo(0, 3)
-    for stage in range(1, last - 1):
-        pass_on(1, stage)
+    pass_on(1, 0)
     if last > 1:
         pass_on(0, last - 1)
     take_halo(0, 2)
@@ -366,17 +365,17 @@
     for group in range(groups):
         field_pass(0, group, 0, 1)
     send_halo(1, 0)
+    for stage in range(1, last - 1):
+        pass_on(1, stage)
     field_pass(0, 0, 1, nz)
     pack_extra(1)
     send_halo(1, 1)
+    for group in range(1, groups):
+        field_pass(0, group, 1, nz)
     if last > 1:
         pass_on(1, last - 1)
-    for group in range(1, groups):
-        field_pass(0, group, 1, nz)
     for group in range(groups - 1):
         dual_pass(1, group, 0, nz - 1)
-    last_copy(1).wait_recv()
-    votes_pass(1, groups - 1, 0, nz)
     take_halo(1, 0)
     take_halo(1, 1)
     for group in range(groups):
@@ -396,8 +395,7 @@
     ]
     for copy in out_dual:
         copy.start()
-    for group in range(groups - 1):
-        votes_pass(1, group, 0, nz)
+    last_copy(1).wait_recv()
     for group in range(1, groups):
         field_pass(1, group, 1, nz)
     take_halo(1, 2)
@@ -430,14 +428,13 @@
     slots = stages + 1
     f32 = jnp.float32
     anywhere = pl.BlockSpec(memory_space=pl.ANY)
-    scalars = pl.BlockSpec(memory_space=pltpu.SMEM)
     return pl.pallas_call(
         functools.partial(kernel, n_slab, n_tile),
         out_shape=(
             jax.ShapeDtypeStruct(field.shape, f32),
             jax.ShapeDtypeStruct(dual.shape, f32),
         ),
-        in_specs=[scalars, scalars, anywhere, anywhere, anywhere],
+        in_specs=[anywhere] * 5,
         out_specs=(anywhere, anywhere),
         scratch_shapes=[
             pltpu.VMEM((ITERS, nz + 1, nx + 8, ny), f32),
@@ -458,13 +455,15 @@
             pltpu.SemaphoreType.DMA((ITERS, slots, 2)),
             pltpu.SemaphoreType.DMA((ITERS, 4)),
             pltpu.SemaphoreType.DMA((ITERS, 4)),
-            pltpu.SemaphoreType.DMA((8,)),
+            pltpu.SemaphoreType.DMA((10,)),
+            pltpu.SMEM(owner.shape, jnp.int32),
+            pltpu.SMEM((ITERS, 1, VIEWS), jnp.int32),
         ],
         compiler_params=pltpu.CompilerParams(
-            collective_id=0, has_side_effects=True, vmem_limit_bytes=40 * 2**20
+            collective_id=0, has_side_effects=True, vmem_limit_bytes=64 * 2**20
         ),
         name="merge",
-    )(owner, visible, field, dual, depth)
+    )(owner, jnp.swapaxes(visible, 1, 2), field, dual, depth)
 
 
 def solution(mesh):

time: 31.6 us -> 29.1 us (0.921)
  the two profiles are of different devices: /device:TPU:1 before, /device:TPU:0 now
where the time goes in v2:
time: 29.1 us; the launch traced here: 28.9 us
  Pallas kernels  23.6 us (81%)
  local copies, waits for them, and re-layouts  4.61 us (16%)
  between operations  0.64 us (2%)
    pallas_call x1, Pallas kernels, per_device(): pl.pallas_call(functools.partial(kernel, n_slab, n_tile), out_shape=(jax....  23.6 us
    unnamed x2, local copies, waits for them, and re-layouts  4.61 us

profile of v2, /device:TPU:0, one launch (start us, length us, event | category | flops | bytes accessed | tf_op | source)
XLA Modules:
  0.0 28.9 jit_solution(17353235036992235816)
XLA Ops:
  0.6 23.6 %merge.1 = (f32[8,16,1024]{2,1,0:T(8,128)}, f32[3,8,16,1024]{3,2,1,0:T(8,128)}) custom-call(s32[2]{0:T(128)} %owner_in.1, s32[2,1,4]{2,1,0:T(1,128)} %bitcast.3, f32[8,16,1024]{2,1,0:T(8,128)} %field_ref.1, f32[3,8,16,1024]{3,2,1,0:T(8,128)} %dual_ref.1, f32[1,2,4,16,1024]{4,3,2,1,0:T(8,128)} %depth_ref.1), custom_call_target="tpu_custom_call" | custom-call | tf_op jit(solution)/shard_map/merge/pallas_call | solution.py:431
  24.2 1.9 %copy.10 = f32[8,16,1024]{2,1,0:T(8,128)} copy(f32[8,16,1024]{2,1,0:T(8,128)} %get-tuple-element.4) | data formatting | bytes 1048576
  26.1 2.7 %copy.11 = f32[3,8,16,1024]{3,2,1,0:T(8,128)} copy(f32[3,8,16,1024]{3,2,1,0:T(8,128)} %get-tuple-element.5) | data formatting | bytes 3145728

commit v3 on v2

--- a/solution.py
+++ b/solution.py
@@ -12,6 +12,7 @@
 BAND = 6
 ITERS = 2
 
+VMEM = 64 * 2**20 - 448 * 1024
 ROWS = 8
 UNIT = 0.35
 HALF = VIEWS // 2
@@ -68,6 +69,25 @@
     first_slab, last_slab = slab == 0, slab == n_slab - 1
     first_tile, last_tile = tile == 0, tile == n_tile - 1
 
+    barrier = pltpu.get_barrier_semaphore()
+    for b in bits:
+        pl.semaphore_signal(
+            barrier, inc=1, device_id={"slab": partner[b]}, device_id_type=MESH
+        )
+    greeted = len(bits)
+    for axis, place, here, there in (
+        ("slab", slab, first_slab, -1),
+        ("slab", slab, last_slab, 1),
+        ("tile", tile, first_tile, -1),
+        ("tile", tile, last_tile, 1),
+    ):
+
+        @pl.when(jnp.logical_not(here))
+        def _(axis=axis, place=place, there=there):
+            pl.semaphore_signal(
+                barrier, inc=1, device_id={axis: place + there}, device_id_type=MESH
+            )
+
     into_field = pltpu.make_async_copy(
         field_ref, extra.at[0, pl.ds(0, nz), pl.ds(0, nx)], local_sem.at[0]
     )
@@ -86,25 +106,6 @@
     into_field.start()
     into_mine[1].start()
     into_dual.start()
-
-    barrier = pltpu.get_barrier_semaphore()
-    for b in bits:
-        pl.semaphore_signal(
-            barrier, inc=1, device_id={"slab": partner[b]}, device_id_type=MESH
-        )
-    greeted = len(bits)
-    for axis, place, here, there in (
-        ("slab", slab, first_slab, -1),
-        ("slab", slab, last_slab, 1),
-        ("tile", tile, first_tile, -1),
-        ("tile", tile, last_tile, 1),
-    ):
-
-        @pl.when(jnp.logical_not(here))
-        def _(axis=axis, place=place, there=there):
-            pl.semaphore_signal(
-                barrier, inc=1, device_id={axis: place + there}, device_id_type=MESH
-            )
 
     inner = [jnp.where(edge, 0, 1) for edge in (first_slab, last_slab, first_tile, last_tile)]
     pl.semaphore_wait(barrier, greeted + inner[0] + inner[1] + inner[2] + inner[3])
@@ -286,12 +287,12 @@
         lax.fori_loop(low, high, body, 0)
 
     def over(low, high, body):
-        def step(i, carry):
-            z = low + lax.div(i, chunks)
-            body(z, pl.ds(pl.multiple_of(lax.rem(i, chunks) * chunk, chunk), chunk))
+        def step(z, carry):
+            for c in range(chunks):
+                body(z, pl.ds(c * chunk, chunk))
             return carry
 
-        lax.fori_loop(0, (high - low) * chunks, step, 0)
+        lax.fori_loop(low, high, step, 0)
 
     def add_votes(k, z, rows, lanes, sums):
         shift = (slab * nz + z).astype(jnp.float32) * (UNIT / BAND)
@@ -327,8 +328,10 @@
                 best = jnp.maximum(
                     best, jnp.minimum(base + (sums[i] - sums[i - 1]), centre)
                 )
-            value[it, z, rows, lanes] = best
-            if it == 0:
+            if it == ITERS - 1:
+                field_out[z, rows, lanes] = best
+            else:
+                value[it, z, rows, lanes] = best
                 extra[1, z, rows, lanes] = 2.0 * best - extra[0, z, rows, lanes]
 
         over(low, high, body)
@@ -403,8 +406,6 @@
     for group in range(groups):
         field_pass(1, group, 0, 1)
     field_pass(1, 0, 1, nz)
-    out_field = pltpu.make_async_copy(value.at[1], field_out, local_sem.at[7])
-    out_field.start()
 
     for k in range(ITERS):
         first_copy(k).wait_send()
@@ -417,7 +418,16 @@
             sent_halo(it, kind)
     for copy in out_dual:
         copy.wait()
-    out_field.wait()
+
+
+def write_out(field_kept, dual_kept, field_out, dual_out, sem):
+    copies = [pltpu.make_async_copy(field_kept, field_out, sem.at[3])]
+    for c in range(3):
+        copies.append(pltpu.make_async_copy(dual_kept.at[c], dual_out.at[c], sem.at[c]))
+    for copy in copies:
+        copy.start()
+    for copy in copies:
+        copy.wait()
 
 
 def per_device(n_slab, n_tile, field, dual, depth, owner, visible):
@@ -428,14 +438,14 @@
     slots = stages + 1
     f32 = jnp.float32
     anywhere = pl.BlockSpec(memory_space=pl.ANY)
-    return pl.pallas_call(
+    field_kept, dual_kept = pl.pallas_call(
         functools.partial(kernel, n_slab, n_tile),
         out_shape=(
-            jax.ShapeDtypeStruct(field.shape, f32),
-            jax.ShapeDtypeStruct(dual.shape, f32),
+            pltpu.VMEM(field.shape, f32),
+            pltpu.VMEM(dual.shape, f32),
         ),
         in_specs=[anywhere] * 5,
-        out_specs=(anywhere, anywhere),
+        out_specs=(pl.BlockSpec(memory_space=pltpu.VMEM),) * 2,
         scratch_shapes=[
             pltpu.VMEM((ITERS, nz + 1, nx + 8, ny), f32),
             pltpu.VMEM((3, nz, nx, ny), f32),
@@ -460,10 +470,21 @@
             pltpu.SMEM((ITERS, 1, VIEWS), jnp.int32),
         ],
         compiler_params=pltpu.CompilerParams(
-            collective_id=0, has_side_effects=True, vmem_limit_bytes=64 * 2**20
+            collective_id=0, has_side_effects=True, vmem_limit_bytes=VMEM - 4 * (field.size + dual.size)
         ),
         name="merge",
     )(owner, jnp.swapaxes(visible, 1, 2), field, dual, depth)
+    return pl.pallas_call(
+        write_out,
+        out_shape=(
+            jax.ShapeDtypeStruct(field.shape, f32),
+            jax.ShapeDtypeStruct(dual.shape, f32),
+        ),
+        in_specs=[pl.BlockSpec(memory_space=pltpu.VMEM)] * 2,
+        out_specs=(anywhere, anywhere),
+        scratch_shapes=[pltpu.SemaphoreType.DMA((4,))],
+        name="write",
+    )(field_kept, dual_kept)
 
 
 def solution(mesh):

time: 29.1 us -> 28.3 us (0.973)
  local copies, waits for them, and re-layouts: 4.61 us -> 1.96 us
  Pallas kernels: 23.6 us -> 25.6 us
    unnamed x2 -> x4, local copies, waits for them, and re-layouts: 4.61 us -> 1.96 us
    pallas_call x1 -> x2, Pallas kernels: 23.6 us -> 25.6 us  [the longest x1 22.6 us: per_device(): pl.pallas_call(functools.partial(kernel, n_slab, n_tile), out_shape=(pltp...]
where the time goes in v3:
time: 28.3 us; the launch traced here: 28.2 us
  Pallas kernels  25.6 us (90%)
  local copies, waits for them, and re-layouts  1.96 us (7%)
  between operations  0.65 us (2%)
    pallas_call x1, Pallas kernels, per_device(): pl.pallas_call(functools.partial(kernel, n_slab, n_tile), out_shape=(pltp...  22.6 us
    pallas_call x1, Pallas kernels, per_device(): pl.pallas_call(write_out, out_shape=(jax.ShapeDtypeStruct(field.shape, f3...  2.92 us
    unnamed x4, local copies, waits for them, and re-layouts  1.96 us

profile of v3, /device:TPU:0, one launch (start us, length us, event | category | flops | bytes accessed | tf_op | source)
XLA Modules:
  0.0 28.2 jit_solution(11123970660744517612)
XLA Ops:
  0.6 22.6 %merge.1 = (f32[8,16,1024]{2,1,0:T(8,128)S(1)}, f32[3,8,16,1024]{3,2,1,0:T(8,128)S(1)}) custom-call(s32[2]{0:T(128)} %owner_in.1, s32[2,1,4]{2,1,0:T(1,128)} %bitcast.3, f32[8,16,1024]{2,1,0:T(8,128)} %field_ref.1, f32[3,8,16,1024]{3,2,1,0:T(8,128)} %dual_ref.1, f32[1,2,4,16,1024]{4,3,2,1,0:T(8,128)} %depth_ref.1), custom_call_target="tpu_custom_call" | custom-call | tf_op jit(solution)/shard_map/merge/pallas_call | solution.py:441
  23.3 0.0 copy-start
  23.3 1.2 %copy-done = f32[3,8,16,1024]{3,2,1,0:T(8,128)} copy-done((f32[3,8,16,1024]{3,2,1,0:T(8,128)}, f32[3,8,16,1024]{3,2,1,0:T(8,128)S(1)}, u32[]{:S(2)}) %copy-start) | copy-done | bytes 1572888
  24.5 0.0 copy-start.1
  24.5 0.8 %copy-done.1 = f32[8,16,1024]{2,1,0:T(8,128)} copy-done((f32[8,16,1024]{2,1,0:T(8,128)}, f32[8,16,1024]{2,1,0:T(8,128)S(1)}, u32[]{:S(2)}) %copy-start.1) | copy-done | bytes 524312
  25.3 2.9 %write.1 = (f32[8,16,1024]{2,1,0:T(8,128)}, f32[3,8,16,1024]{3,2,1,0:T(8,128)}) custom-call(f32[8,16,1024]{2,1,0:T(8,128)} %copy-done.1, f32[3,8,16,1024]{3,2,1,0:T(8,128)} %copy-done), custom_call_target="tpu_custom_call" | custom-call | tf_op jit(solution)/shard_map/write/pallas_call | solution.py:477
Async XLA Ops:
  23.3 1.2 %copy-start = (f32[3,8,16,1024]{3,2,1,0:T(8,128)}, f32[3,8,16,1024]{3,2,1,0:T(8,128)S(1)}, u32[]{:S(2)}) copy-start(f32[3,8,16,1024]{3,2,1,0:T(8,128)S(1)} %get-tuple-element.5.dual_kept) | copy-start | bytes 4718596
  24.5 0.8 %copy-start.1 = (f32[8,16,1024]{2,1,0:T(8,128)}, f32[8,16,1024]{2,1,0:T(8,128)S(1)}, u32[]{:S(2)}) copy-start(f32[8,16,1024]{2,1,0:T(8,128)S(1)} %get-tuple-element.4.field_kept) | copy-start | bytes 1572868

commit v4 on v3

--- a/solution.py
+++ b/solution.py
@@ -483,6 +483,7 @@
         in_specs=[pl.BlockSpec(memory_space=pltpu.VMEM)] * 2,
         out_specs=(anywhere, anywhere),
         scratch_shapes=[pltpu.SemaphoreType.DMA((4,))],
+        compiler_params=pltpu.CompilerParams(vmem_limit_bytes=4 * 2**20),
         name="write",
     )(field_kept, dual_kept)
 

time: 28.3 us -> 24.8 us (0.88)
  local copies, waits for them, and re-layouts: 1.96 us -> 0 us
  Pallas kernels: 25.6 us -> 24 us
    unnamed x4 -> x0, local copies, waits for them, and re-layouts: 1.96 us -> none
    pallas_call x1, Pallas kernels: 2.92 us -> 1.35 us  [per_device(): pl.pallas_call(write_out, out_shape=(jax.ShapeDtypeStruct(field.shape, f3...]
where the time goes in v4:
time: 24.8 us; the launch traced here: 24.6 us
  Pallas kernels  24 us (97%)
  between operations  0.64 us (3%)
    pallas_call x1, Pallas kernels, per_device(): pl.pallas_call(functools.partial(kernel, n_slab, n_tile), out_shape=(pltp...  22.6 us
    pallas_call x1, Pallas kernels, per_device(): pl.pallas_call(write_out, out_shape=(jax.ShapeDtypeStruct(field.shape, f3...  1.35 us

profile of v4, /device:TPU:0, one launch (start us, length us, event | category | flops | bytes accessed | tf_op | source)
XLA Modules:
  0.0 24.6 jit_solution(472989081935398088)
XLA Ops:
  0.6 22.6 %merge.1 = (f32[8,16,1024]{2,1,0:T(8,128)S(1)}, f32[3,8,16,1024]{3,2,1,0:T(8,128)S(1)}) custom-call(s32[2]{0:T(128)} %owner_in.1, s32[2,1,4]{2,1,0:T(1,128)} %bitcast.3, f32[8,16,1024]{2,1,0:T(8,128)} %field_ref.1, f32[3,8,16,1024]{3,2,1,0:T(8,128)} %dual_ref.1, f32[1,2,4,16,1024]{4,3,2,1,0:T(8,128)} %depth_ref.1), custom_call_target="tpu_custom_call" | custom-call | tf_op jit(solution)/shard_map/merge/pallas_call | solution.py:441
  23.3 1.3 %write.1 = (f32[8,16,1024]{2,1,0:T(8,128)}, f32[3,8,16,1024]{3,2,1,0:T(8,128)}) custom-call(f32[8,16,1024]{2,1,0:T(8,128)S(1)} %get-tuple-element.4.field_kept, f32[3,8,16,1024]{3,2,1,0:T(8,128)S(1)} %get-tuple-element.5.dual_kept), custom_call_target="tpu_custom_call" | custom-call | tf_op jit(solution)/shard_map/write/pallas_call | solution.py:477

commit v5 on v4

--- a/solution.py
+++ b/solution.py
@@ -53,7 +53,7 @@
 ):
     nz, nx, ny = field_ref.shape
     groups = nx // ROWS
-    chunk = min(512, ny)
+    chunk = min(256, ny)
     chunks = ny // chunk
     slab = lax.axis_index("slab")
     tile = lax.axis_index("tile")

time: 24.8 us -> 24.8 us (level)
  no operation moved by 1% of the time
where the time goes in v5:
time: 24.8 us; the launch traced here: 24.6 us
  Pallas kernels  24 us (97%)
  between operations  0.64 us (3%)
    pallas_call x1, Pallas kernels, per_device(): pl.pallas_call(functools.partial(kernel, n_slab, n_tile), out_shape=(pltp...  22.6 us
    pallas_call x1, Pallas kernels, per_device(): pl.pallas_call(write_out, out_shape=(jax.ShapeDtypeStruct(field.shape, f3...  1.35 us

profile of v5, /device:TPU:0, one launch (start us, length us, event | category | flops | bytes accessed | tf_op | source)
XLA Modules:
  0.0 24.6 jit_solution(5564276393777788236)
XLA Ops:
  0.6 22.6 %merge.1 = (f32[8,16,1024]{2,1,0:T(8,128)S(1)}, f32[3,8,16,1024]{3,2,1,0:T(8,128)S(1)}) custom-call(s32[2]{0:T(128)} %owner_in.1, s32[2,1,4]{2,1,0:T(1,128)} %bitcast.3, f32[8,16,1024]{2,1,0:T(8,128)} %field_ref.1, f32[3,8,16,1024]{3,2,1,0:T(8,128)} %dual_ref.1, f32[1,2,4,16,1024]{4,3,2,1,0:T(8,128)} %depth_ref.1), custom_call_target="tpu_custom_call" | custom-call | tf_op jit(solution)/shard_map/merge/pallas_call | solution.py:441
  23.3 1.3 %write.1 = (f32[8,16,1024]{2,1,0:T(8,128)}, f32[3,8,16,1024]{3,2,1,0:T(8,128)}) custom-call(f32[8,16,1024]{2,1,0:T(8,128)S(1)} %get-tuple-element.4.field_kept, f32[3,8,16,1024]{3,2,1,0:T(8,128)S(1)} %get-tuple-element.5.dual_kept), custom_call_target="tpu_custom_call" | custom-call | tf_op jit(solution)/shard_map/write/pallas_call | solution.py:477
